TPU v7x, 32 devices: a whole 2x2x4 slice. The times are simulated.
32 devices in a mesh: groups: 2 (over y), src: 16 (over z, x, core).
Axes of the slice: x: 2, y: 2, z: 4, core: 2. Of those that a mesh axis runs over, the one named last changes fastest.
Arguments:
- src_points: bfloat16 [256, 64, 256], P(('groups', 'src')), parts along dimension 0, may hold values from -1.5 to 1.5
- tgt_points: bfloat16 [256, 64, 256], P(('groups', 'src')), parts along dimension 0, may hold values from -1.5 to 1.5
- g_init: float32 [256, 256], P(('groups', 'src')), parts along dimension 0, may hold values from 2 to 66
- far_src: float32 [256, 256], P(('groups', 'src')), parts along dimension 0, may hold values from 10 to 22
- far_tgt: float32 [256, 256], P(('groups', 'src')), parts along dimension 0, may hold values from -160 to -14
- cand_owner: int32 [256, 8], P(('groups', 'src')), parts along dimension 0, may hold values from 0 to 15, all different within a row; in each aligned block of 8 rows (0 to 7, 8 to 15, ...) at most 4 rows name the same one
- cand_local: int32 [256, 8], P(('groups', 'src')), parts along dimension 0, may hold values from 0 to 7
Outputs:
- src_potential: float32 [256, 256], P(('groups', 'src')), parts along dimension 0
- tgt_potential: float32 [256, 256], P(('groups', 'src')), parts along dimension 0
There are 2 independent parts, one for each index of `groups`. A program takes and returns all parts, laid end to end along the dimension named above; each array names one. Nothing has to cross between parts.
Inputs may be any that keep to these rules, and one draw needn't show every extreme that they name: `cand_owner`: each source cluster names 8 different shards; among the 8 source clusters of one device at most 4 name the same shard, and in every draw some device names some shard exactly 4 times.
All inputs are finite; a program needn't handle non-finite values.
Results may differ from a plain program's by a relative error of at most 0.0003.
Values may be sent and summed in bfloat16 or wider, within the bound.
A program may use at most 64 MiB of HBM per device.

v0:
```python
import jax
import jax.numpy as jnp
from jax import lax
from jax.sharding import PartitionSpec as P

ITERS = 2


SCALE_EPS = 0.25
KEEP_TAU = 0.8
VERY_LOW = -1e30


def half_norms(blocks):
    wide = blocks.astype(jnp.float32)
    return 0.5 * jnp.sum(wide * wide, axis=-2)


def per_device(src_points, tgt_points, g_init, far_src, far_tgt, cand_owner, cand_local):
    src_count, feature_dim, cluster_size = src_points.shape
    tgt_count = tgt_points.shape[0]
    per_cluster = cand_owner.shape[1]
    shards = lax.axis_size("src")
    capacity = max(2, min(src_count // 2, 2 * src_count * per_cluster // shards))
    requests = src_count * per_cluster
    slot_count = shards * capacity
    group_size = 4
    group_count = src_count // group_size
    owners = cand_owner.reshape(requests)
    wanted = cand_local.reshape(requests)
    onehot = (owners[:, None] == jnp.arange(shards, dtype=jnp.int32)[None, :]).astype(jnp.int32)
    earlier = jnp.cumsum(onehot, axis=0) - onehot
    within = jnp.sum(earlier * onehot, axis=1)
    slot_pos = owners * capacity + within
    request_table = jnp.full((slot_count,), -1, jnp.int32).at[slot_pos].set(wanted)
    asked_ids = lax.all_to_all(
        request_table.reshape(shards, capacity), "src", split_axis=0, concat_axis=0, tiled=True
    ).reshape(slot_count)
    safe_ids = jnp.maximum(asked_ids, 0)
    member = (asked_ids[:, None] == jnp.arange(tgt_count, dtype=jnp.int32)[None, :]).astype(
        jnp.float32
    )
    member_rows = member.T
    send_points = tgt_points[safe_ids].reshape(shards, capacity, feature_dim, cluster_size)
    src_half = half_norms(src_points)
    src_grouped = src_points.reshape(group_count, group_size, feature_dim, cluster_size)
    half_grouped = src_half.reshape(group_count, group_size, cluster_size)
    far_grouped = far_src.reshape(group_count, group_size, cluster_size)

    def tile_cost(src_block, src_norm, tgt_block, tgt_norm):
        inner = jnp.einsum(
            "gdp,gkdq->gpkq", src_block, tgt_block, preferred_element_type=jnp.float32
        )
        return src_norm[:, :, None, None] + tgt_norm[:, None, :, :] - inner

    def row_pass(blocks, block_half, req_pot):

        def row_one_group(pieces):
            src_block, src_norm, tgt_block, tgt_norm, tgt_values, far_term = pieces
            cost = tile_cost(src_block, src_norm, tgt_block, tgt_norm)
            scores = (tgt_values[:, None, :, :] - cost) / SCALE_EPS
            highest = jnp.maximum(jnp.max(scores, axis=(2, 3)), far_term)
            total = jnp.exp(far_term - highest) + jnp.sum(
                jnp.exp(scores - highest[:, :, None, None]), axis=(2, 3)
            )
            return -KEEP_TAU * SCALE_EPS * (highest + jnp.log(total))

        pieces = (
            src_grouped,
            half_grouped,
            blocks.reshape(group_count, group_size, per_cluster, feature_dim, cluster_size),
            block_half.reshape(group_count, group_size, per_cluster, cluster_size),
            req_pot.reshape(group_count, group_size, per_cluster, cluster_size),
            far_grouped,
        )
        return lax.map(row_one_group, pieces).reshape(src_count, cluster_size)

    def column_pass(blocks, block_half, src_pot):

        def column_one_group(pieces):
            src_block, src_norm, tgt_block, tgt_norm, src_values = pieces
            cost = tile_cost(src_block, src_norm, tgt_block, tgt_norm)
            scores = (src_values[:, :, None, None] - cost) / SCALE_EPS
            highest = jnp.max(scores, axis=1)
            total = jnp.sum(jnp.exp(scores - highest[:, None, :, :]), axis=1)
            return (highest, total)

        pieces = (
            src_grouped,
            half_grouped,
            blocks.reshape(group_count, group_size, per_cluster, feature_dim, cluster_size),
            block_half.reshape(group_count, group_size, per_cluster, cluster_size),
            src_pot.reshape(group_count, group_size, cluster_size),
        )
        col_high, col_total = lax.map(column_one_group, pieces)
        col_high = col_high.reshape(requests, cluster_size)
        col_total = col_total.reshape(requests, cluster_size)
        send_high = (
            jnp.full((slot_count, cluster_size), VERY_LOW, jnp.float32).at[slot_pos].set(col_high)
        )
        send_total = jnp.zeros((slot_count, cluster_size), jnp.float32).at[slot_pos].set(col_total)
        back_high, back_total = (
            lax.all_to_all(
                send_high.reshape(shards, capacity, cluster_size),
                "src",
                split_axis=0,
                concat_axis=0,
                tiled=True,
            ),
            lax.all_to_all(
                send_total.reshape(shards, capacity, cluster_size),
                "src",
                split_axis=0,
                concat_axis=0,
                tiled=True,
            ),
        )
        back_high = back_high.reshape(slot_count, cluster_size)
        back_total = back_total.reshape(slot_count, cluster_size)

        def cluster_best(column):
            return jnp.max(jnp.where(column[:, None] > 0.5, back_high, VERY_LOW), axis=0)

        best = jnp.maximum(far_tgt, lax.map(cluster_best, member_rows))
        weights = back_total * jnp.exp(back_high - best[safe_ids])
        summed = jnp.exp(far_tgt - best) + jnp.dot(
            member_rows, weights, precision=lax.Precision.HIGHEST
        )
        return -KEEP_TAU * SCALE_EPS * (best + jnp.log(summed))

    tgt_pot = g_init
    src_pot = jnp.zeros((src_count, cluster_size), jnp.float32)
    for iteration in range(ITERS):
        flattened = lax.all_to_all(
            send_points, "src", split_axis=0, concat_axis=0, tiled=True
        ).reshape(slot_count, feature_dim, cluster_size)
        chosen = flattened[slot_pos]
        blocks = chosen
        block_half = half_norms(chosen)
        send_pot = tgt_pot[safe_ids].reshape(shards, capacity, cluster_size)
        got_pot = lax.all_to_all(send_pot, "src", split_axis=0, concat_axis=0, tiled=True)
        req_pot = got_pot.reshape(slot_count, cluster_size)[slot_pos]
        src_pot = row_pass(blocks, block_half, req_pot)
        tgt_pot = column_pass(blocks, block_half, src_pot)
    return (src_pot, tgt_pot)


def solution(mesh):
    return jax.shard_map(
        per_device,
        mesh=mesh,
        in_specs=(
            P(("groups", "src"), None, None),
            P(("groups", "src"), None, None),
            P(("groups", "src"), None),
            P(("groups", "src"), None),
            P(("groups", "src"), None),
            P(("groups", "src"), None),
            P(("groups", "src"), None),
        ),
        out_specs=(P(("groups", "src"), None), P(("groups", "src"), None)),
        check_vma=False,
    )
```

profile of v0, /device:TPU:0, one launch (start us, length us, event | category | flops | bytes accessed | tf_op | source)
XLA Modules:
  0.0 192.3 jit_solution(4724374246698592759)
XLA Ops:
  4.3 13.6 %all_to_all.45 = s32[16,1,4]{2,1,0:T(1,128)S(1)} all-to-all(s32[16,1,4]{2,1,0:T(1,128)S(1)} %bitcast.212), channel_id=1, replica_groups=mesh['groups'=2,'src'=16] {'src'}, dimensions={0} | all-to-all | bytes 512 | tf_op jit(solution)/shard_map/all_to_all | solution.py:36
  21.1 3.5 %all-to-all-start.1 = ((f32[16,4,256]{2,1,0:T(4,128)}), f32[16,4,256]{2,1,0:T(4,128)S(1)}, u32[]{:S(2)}, u32[]{:S(2)}) async-start(f32[16,4,256]{2,1,0:T(4,128)} %reshape.209), calls=%async_computation.1 | async-start | bytes 131072 | tf_op jit(solution)/shard_map/all_to_all | solution.py:141
  26.7 4.8 %all-to-all-done.1 = f32[16,4,256]{2,1,0:T(4,128)S(1)} async-done(((f32[16,4,256]{2,1,0:T(4,128)}), f32[16,4,256]{2,1,0:T(4,128)S(1)}, u32[]{:S(2)}, u32[]{:S(2)}) %all-to-all-start.1) | async-done | bytes 65568 | tf_op jit(solution)/shard_map/all_to_all | solution.py:141
  31.5 3.7 %all-to-all-start.2 = ((bf16[16,4,64,256]{3,2,1,0:T(8,128)(2,1)}), bf16[16,4,64,256]{3,2,1,0:T(8,128)(2,1)S(1)}, u32[]{:S(2)}, u32[]{:S(2)}) async-start(bf16[16,4,64,256]{3,2,1,0:T(8,128)(2,1)} %bitcast.46), calls=%async_computation.2 | async-start | bytes 4194304 | tf_op jit(solution)/shard_map/all_to_all | solution.py:134
  36.1 40.1 %all-to-all-done.2 = bf16[16,4,64,256]{3,2,1,0:T(8,128)(2,1)S(1)} async-done(((bf16[16,4,64,256]{3,2,1,0:T(8,128)(2,1)}), bf16[16,4,64,256]{3,2,1,0:T(8,128)(2,1)S(1)}, u32[]{:S(2)}, u32[]{:S(2)}) %all-to-all-start.2) | async-done | bytes 2097184 | tf_op jit(solution)/shard_map/all_to_all | solution.py:134
  77.6 2.3 %gather_fusion.3 = bf16[64,64,256]{2,1,0:T(8,128)(2,1)S(1)} fusion(bf16[64,64,256]{2,1,0:T(8,128)(2,1)} %bitcast.201, s32[1024]{0:T(1024)S(1)} %pad_clamp_fusion), kind=kCustom, calls=%fused_computation.3 | custom fusion | bytes 4194560 | tf_op jit(solution)/shard_map/gather | solution.py:137
  80.6 11.7 %while.64 = (s32[]{:T(128)}, f32[2,4,256]{2,1,0:T(4,128)S(1)}, f32[2,4,8,256]{3,2,1,0:T(8,128)S(1)}, f32[2,4,256]{2,1,0:T(4,128)S(1)}, f32[2,4,8,256]{3,2,1,0:T(...) while((s32[]{:T(128)}, f32[2,4,256]{2,1,0:T(4,128)S(1)}, ...), condition=%wide.region_8.9_spmd, body=%wide.region_5.8_spmd.sunk | while | flops 291508224 | bytes 18277484 | solution.py:76
  80.6 3.2 %fusion.69 = (f32[4,256]{1,0:T(4,128)S(1)}, f32[4,256,8,256]{1,3,2,0:T(8,128)S(1)}) fusion(f32[4,8,256]{2,1,0:T(8,128)S(1)} %get-tuple-element.552, f32[4,256]{1,0:T(4,128)S(1)} %dynamic-slice_bitcast_fusion.23, f32[4,8,256]{2,1,0:T(8,128)S(1)} %get-tuple-element.553, bf16[2,4,8,64,256]{4,3,2,1,0:T(8,128)(2,1)S(1)} %get-tuple-element.624, ...), kind=kOutput, calls=%fused_computation.15.clone.1 | convolution fusion | flops 278920192 | bytes 9643008 | tf_op jit(solution)/shard_map/while/body/eval_jaxpr/gdp,gkdq->gpkq/dot_general | solution.py:51
  83.8 2.6 %exponential_reduce_fusion.8 = f32[4,256]{1,0:T(4,128)S(1)} fusion(f32[4,256,8,256]{1,3,2,0:T(8,128)S(1)} %get-tuple-element.554, f32[4,256]{1,0:T(4,128)S(1)} %bitcast_maximum_fusion.6, f32[4,8,256]{2,1,0:T(8,128)S(1)} %get-tuple-element.552, f32[4,256]{1,0:T(4,128)S(1)} %dynamic-slice_bitcast_fusion.23, f32[4,8,256]{2,1,0:T(8,128)S(1)} %get-tuple-element.553), kind=kLoop, calls=%fused_computation.13.clone.1 | loop fusion | flops 12581888 | bytes 8466432 | tf_op jit(solution)/shard_map/while/body/eval_jaxpr/reduce_sum | solution.py:63
  86.5 3.2 %fusion.69 = (f32[4,256]{1,0:T(4,128)S(1)}, f32[4,256,8,256]{1,3,2,0:T(8,128)S(1)}) fusion(f32[4,8,256]{2,1,0:T(8,128)S(1)} %get-tuple-element.552, f32[4,256]{1,0:T(4,128)S(1)} %dynamic-slice_bitcast_fusion.23, f32[4,8,256]{2,1,0:T(8,128)S(1)} %get-tuple-element.553, bf16[2,4,8,64,256]{4,3,2,1,0:T(8,128)(2,1)S(1)} %get-tuple-element.624, ...), kind=kOutput, calls=%fused_computation.15.clone.1 | convolution fusion | flops 278920192 | bytes 9643008 | tf_op jit(solution)/shard_map/while/body/eval_jaxpr/gdp,gkdq->gpkq/dot_general | solution.py:51
  89.6 2.6 %exponential_reduce_fusion.8 = f32[4,256]{1,0:T(4,128)S(1)} fusion(f32[4,256,8,256]{1,3,2,0:T(8,128)S(1)} %get-tuple-element.554, f32[4,256]{1,0:T(4,128)S(1)} %bitcast_maximum_fusion.6, f32[4,8,256]{2,1,0:T(8,128)S(1)} %get-tuple-element.552, f32[4,256]{1,0:T(4,128)S(1)} %dynamic-slice_bitcast_fusion.23, f32[4,8,256]{2,1,0:T(8,128)S(1)} %get-tuple-element.553), kind=kLoop, calls=%fused_computation.13.clone.1 | loop fusion | flops 12581888 | bytes 8466432 | tf_op jit(solution)/shard_map/while/body/eval_jaxpr/reduce_sum | solution.py:63
  92.3 11.3 %while.65 = (s32[]{:T(128)}, f32[2,4,8,256]{3,2,1,0:T(8,128)S(1)}, f32[2,4,8,256]{3,2,1,0:T(8,128)S(1)}, f32[2,4,256]{2,1,0:T(4,128)S(1)}, f32[2,4,256]{2,1,0:T(...) while((s32[]{:T(128)}, f32[2,4,8,256]{3,2,1,0:T(8,128)S(1)}, ...), condition=%wide.region_12.13_spmd, body=%wide.region_9.12_spmd.sunk | while | flops 291487744 | bytes 18351212 | solution.py:95
  94.4 3.6 %exponential_reduce_fusion.9 = f32[4,8,256]{2,1,0:T(8,128)S(1)} fusion(f32[4,256,8,256]{3,1,2,0:T(8,128)S(1)} %get-tuple-element.564, f32[4,8,256]{2,1,0:T(8,128)S(1)} %get-tuple-element.565, f32[4,8,256]{2,1,0:T(8,128)S(1)} %dynamic-slice_bitcast_fusion.24, f32[4,256]{1,0:T(4,128)S(1)} %dynamic-slice_bitcast_fusion.25, ...), kind=kLoop, calls=%fused_computation.32.clone.1 | loop fusion | flops 12574720 | bytes 8495104 | tf_op jit(solution)/shard_map/while/body/eval_jaxpr/reduce_sum | solution.py:85
  100.0 3.6 %exponential_reduce_fusion.9 = f32[4,8,256]{2,1,0:T(8,128)S(1)} fusion(f32[4,256,8,256]{3,1,2,0:T(8,128)S(1)} %get-tuple-element.564, f32[4,8,256]{2,1,0:T(8,128)S(1)} %get-tuple-element.565, f32[4,8,256]{2,1,0:T(8,128)S(1)} %dynamic-slice_bitcast_fusion.24, f32[4,256]{1,0:T(4,128)S(1)} %dynamic-slice_bitcast_fusion.25, ...), kind=kLoop, calls=%fused_computation.32.clone.1 | loop fusion | flops 12574720 | bytes 8495104 | tf_op jit(solution)/shard_map/while/body/eval_jaxpr/reduce_sum | solution.py:85
  105.1 11.2 %all-to-all-start.3 = ((f32[16,4,256]{2,1,0:T(4,128)}), f32[16,4,256]{2,1,0:T(4,128)S(1)}, u32[]{:S(2)}, u32[]{:S(2)}) async-start(f32[16,4,256]{2,1,0:T(4,128)} %reshape.218), calls=%async_computation.3 | async-start | bytes 131072 | tf_op jit(solution)/shard_map/all_to_all | solution.py:103
  117.8 5.4 %all-to-all-done.3 = f32[16,4,256]{2,1,0:T(4,128)S(1)} async-done(((f32[16,4,256]{2,1,0:T(4,128)}), f32[16,4,256]{2,1,0:T(4,128)S(1)}, u32[]{:S(2)}, u32[]{:S(2)}) %all-to-all-start.3) | async-done | bytes 65568 | tf_op jit(solution)/shard_map/all_to_all | solution.py:103
  123.2 3.5 %all-to-all-start.4 = ((f32[16,4,256]{2,1,0:T(4,128)}), f32[16,4,256]{2,1,0:T(4,128)S(1)}, u32[]{:S(2)}, u32[]{:S(2)}) async-start(f32[16,4,256]{2,1,0:T(4,128)} %reshape.221), calls=%async_computation.4 | async-start | bytes 131072 | tf_op jit(solution)/shard_map/all_to_all | solution.py:110
  128.8 4.8 %all-to-all-done.4 = f32[16,4,256]{2,1,0:T(4,128)S(1)} async-done(((f32[16,4,256]{2,1,0:T(4,128)}), f32[16,4,256]{2,1,0:T(4,128)S(1)}, u32[]{:S(2)}, u32[]{:S(2)}) %all-to-all-start.4) | async-done | bytes 65568 | tf_op jit(solution)/shard_map/all_to_all | solution.py:110
  135.2 3.7 %all-to-all-start.5 = ((f32[16,4,256]{2,1,0:T(4,128)}), f32[16,4,256]{2,1,0:T(4,128)S(1)}, u32[]{:S(2)}, u32[]{:S(2)}) async-start(f32[16,4,256]{2,1,0:T(4,128)} %reshape.223), calls=%async_computation.5 | async-start | bytes 131072 | tf_op jit(solution)/shard_map/all_to_all | solution.py:141
  138.8 6.7 %all-to-all-done.5 = f32[16,4,256]{2,1,0:T(4,128)S(1)} async-done(((f32[16,4,256]{2,1,0:T(4,128)}), f32[16,4,256]{2,1,0:T(4,128)S(1)}, u32[]{:S(2)}, u32[]{:S(2)}) %all-to-all-start.5) | async-done | bytes 65568 | tf_op jit(solution)/shard_map/all_to_all | solution.py:141
  146.2 11.7 %while.67 = (s32[]{:T(128)}, f32[2,4,256]{2,1,0:T(4,128)S(1)}, f32[2,4,8,256]{3,2,1,0:T(8,128)S(1)}, f32[2,4,256]{2,1,0:T(4,128)S(1)}, f32[2,4,8,256]{3,2,1,0:T(...) while((s32[]{:T(128)}, f32[2,4,256]{2,1,0:T(4,128)S(1)}, ...), condition=%wide.region_21.22_spmd, body=%wide.region_18.21_spmd.sunk | while | flops 291508224 | bytes 18277484 | solution.py:76
  146.3 3.2 %fusion.72 = (f32[4,256]{1,0:T(4,128)S(1)}, f32[4,256,8,256]{1,3,2,0:T(8,128)S(1)}) fusion(f32[4,8,256]{2,1,0:T(8,128)S(1)} %get-tuple-element.580, f32[4,256]{1,0:T(4,128)S(1)} %dynamic-slice_bitcast_fusion.28, f32[4,8,256]{2,1,0:T(8,128)S(1)} %get-tuple-element.581, bf16[2,4,8,64,256]{4,3,2,1,0:T(8,128)(2,1)S(1)} %get-tuple-element.696, ...), kind=kOutput, calls=%fused_computation.50.clone.1 | convolution fusion | flops 278920192 | bytes 9643008 | tf_op jit(solution)/shard_map/while/body/eval_jaxpr/gdp,gkdq->gpkq/dot_general | solution.py:51
  149.4 2.6 %exponential_reduce_fusion.10 = f32[4,256]{1,0:T(4,128)S(1)} fusion(f32[4,256,8,256]{1,3,2,0:T(8,128)S(1)} %get-tuple-element.582, f32[4,256]{1,0:T(4,128)S(1)} %bitcast_maximum_fusion.7, f32[4,8,256]{2,1,0:T(8,128)S(1)} %get-tuple-element.580, f32[4,256]{1,0:T(4,128)S(1)} %dynamic-slice_bitcast_fusion.28, f32[4,8,256]{2,1,0:T(8,128)S(1)} %get-tuple-element.581), kind=kLoop, calls=%fused_computation.48.clone.1 | loop fusion | flops 12581888 | bytes 8466432 | tf_op jit(solution)/shard_map/while/body/eval_jaxpr/reduce_sum | solution.py:63
  152.1 3.2 %fusion.72 = (f32[4,256]{1,0:T(4,128)S(1)}, f32[4,256,8,256]{1,3,2,0:T(8,128)S(1)}) fusion(f32[4,8,256]{2,1,0:T(8,128)S(1)} %get-tuple-element.580, f32[4,256]{1,0:T(4,128)S(1)} %dynamic-slice_bitcast_fusion.28, f32[4,8,256]{2,1,0:T(8,128)S(1)} %get-tuple-element.581, bf16[2,4,8,64,256]{4,3,2,1,0:T(8,128)(2,1)S(1)} %get-tuple-element.696, ...), kind=kOutput, calls=%fused_computation.50.clone.1 | convolution fusion | flops 278920192 | bytes 9643008 | tf_op jit(solution)/shard_map/while/body/eval_jaxpr/gdp,gkdq->gpkq/dot_general | solution.py:51
  155.3 2.6 %exponential_reduce_fusion.10 = f32[4,256]{1,0:T(4,128)S(1)} fusion(f32[4,256,8,256]{1,3,2,0:T(8,128)S(1)} %get-tuple-element.582, f32[4,256]{1,0:T(4,128)S(1)} %bitcast_maximum_fusion.7, f32[4,8,256]{2,1,0:T(8,128)S(1)} %get-tuple-element.580, f32[4,256]{1,0:T(4,128)S(1)} %dynamic-slice_bitcast_fusion.28, f32[4,8,256]{2,1,0:T(8,128)S(1)} %get-tuple-element.581), kind=kLoop, calls=%fused_computation.48.clone.1 | loop fusion | flops 12581888 | bytes 8466432 | tf_op jit(solution)/shard_map/while/body/eval_jaxpr/reduce_sum | solution.py:63
  157.9 11.3 %while.68 = (s32[]{:T(128)}, f32[2,4,8,256]{3,2,1,0:T(8,128)S(1)}, f32[2,4,8,256]{3,2,1,0:T(8,128)S(1)}, f32[2,4,256]{2,1,0:T(4,128)S(1)}, f32[2,4,256]{2,1,0:T(...) while((s32[]{:T(128)}, f32[2,4,8,256]{3,2,1,0:T(8,128)S(1)}, ...), condition=%wide.region_25.26_spmd, body=%wide.region_22.25_spmd.sunk | while | flops 291487744 | bytes 18351212 | solution.py:95
  160.0 3.6 %exponential_reduce_fusion.11 = f32[4,8,256]{2,1,0:T(8,128)S(1)} fusion(f32[4,256,8,256]{3,1,2,0:T(8,128)S(1)} %get-tuple-element.592, f32[4,8,256]{2,1,0:T(8,128)S(1)} %get-tuple-element.593, f32[4,8,256]{2,1,0:T(8,128)S(1)} %dynamic-slice_bitcast_fusion.29, f32[4,256]{1,0:T(4,128)S(1)} %dynamic-slice_bitcast_fusion.30, ...), kind=kLoop, calls=%fused_computation.67.clone.1 | loop fusion | flops 12574720 | bytes 8495104 | tf_op jit(solution)/shard_map/while/body/eval_jaxpr/reduce_sum | solution.py:85
  165.6 3.6 %exponential_reduce_fusion.11 = f32[4,8,256]{2,1,0:T(8,128)S(1)} fusion(f32[4,256,8,256]{3,1,2,0:T(8,128)S(1)} %get-tuple-element.592, f32[4,8,256]{2,1,0:T(8,128)S(1)} %get-tuple-element.593, f32[4,8,256]{2,1,0:T(8,128)S(1)} %dynamic-slice_bitcast_fusion.29, f32[4,256]{1,0:T(4,128)S(1)} %dynamic-slice_bitcast_fusion.30, ...), kind=kLoop, calls=%fused_computation.67.clone.1 | loop fusion | flops 12574720 | bytes 8495104 | tf_op jit(solution)/shard_map/while/body/eval_jaxpr/reduce_sum | solution.py:85
  170.7 3.5 %all-to-all-start.6 = ((f32[16,4,256]{2,1,0:T(4,128)}), f32[16,4,256]{2,1,0:T(4,128)S(1)}, u32[]{:S(2)}, u32[]{:S(2)}) async-start(f32[16,4,256]{2,1,0:T(4,128)} %reshape.228), calls=%async_computation.6 | async-start | bytes 131072 | tf_op jit(solution)/shard_map/all_to_all | solution.py:103
  176.3 4.8 %all-to-all-done.6 = f32[16,4,256]{2,1,0:T(4,128)S(1)} async-done(((f32[16,4,256]{2,1,0:T(4,128)}), f32[16,4,256]{2,1,0:T(4,128)S(1)}, u32[]{:S(2)}, u32[]{:S(2)}) %all-to-all-start.6) | async-done | bytes 65568 | tf_op jit(solution)/shard_map/all_to_all | solution.py:103
  181.1 3.5 %all-to-all-start.7 = ((f32[16,4,256]{2,1,0:T(4,128)}), f32[16,4,256]{2,1,0:T(4,128)S(1)}, u32[]{:S(2)}, u32[]{:S(2)}) async-start(f32[16,4,256]{2,1,0:T(4,128)} %reshape.231), calls=%async_computation.7 | async-start | bytes 131072 | tf_op jit(solution)/shard_map/all_to_all | solution.py:110
  186.6 4.8 %all-to-all-done.7 = f32[16,4,256]{2,1,0:T(4,128)S(1)} async-done(((f32[16,4,256]{2,1,0:T(4,128)}), f32[16,4,256]{2,1,0:T(4,128)S(1)}, u32[]{:S(2)}, u32[]{:S(2)}) %all-to-all-start.7) | async-done | bytes 65568 | tf_op jit(solution)/shard_map/all_to_all | solution.py:110
  (155 shorter events, 36.2 us)
Async XLA Ops:
  0.6 24.0 %copy-start = (bf16[8,64,256]{2,1,0:T(8,128)(2,1)S(1)}, bf16[8,64,256]{2,1,0:T(8,128)(2,1)}, u32[]{:S(2)}) copy-start(bf16[8,64,256]{2,1,0:T(8,128)(2,1)} %param.20) | copy-start | bytes 786436
  0.6 34.6 %copy-start.2 = (bf16[8,64,256]{2,1,0:T(8,128)(2,1)S(1)}, bf16[8,64,256]{2,1,0:T(8,128)(2,1)}, u32[]{:S(2)}) copy-start(bf16[8,64,256]{2,1,0:T(8,128)(2,1)} %param.19) | copy-start | bytes 786436
  0.7 34.7 %copy-start.4 = (f32[8,256]{1,0:T(8,128)S(1)}, f32[8,256]{1,0:T(8,128)}, u32[]{:S(2)}) copy-start(f32[8,256]{1,0:T(8,128)} %param.22) | copy-start | bytes 24580
  21.1 10.4 %all-to-all-start.1 = ((f32[16,4,256]{2,1,0:T(4,128)}), f32[16,4,256]{2,1,0:T(4,128)S(1)}, u32[]{:S(2)}, u32[]{:S(2)}) async-start(f32[16,4,256]{2,1,0:T(4,128)} %reshape.209), calls=%async_computation.1 | async-start | bytes 131072 | tf_op jit(solution)/shard_map/all_to_all | solution.py:141
  31.5 44.8 %all-to-all-start.2 = ((bf16[16,4,64,256]{3,2,1,0:T(8,128)(2,1)}), bf16[16,4,64,256]{3,2,1,0:T(8,128)(2,1)S(1)}, u32[]{:S(2)}, u32[]{:S(2)}) async-start(bf16[16,4,64,256]{3,2,1,0:T(8,128)(2,1)} %bitcast.46), calls=%async_computation.2 | async-start | bytes 4194304 | tf_op jit(solution)/shard_map/all_to_all | solution.py:134
  76.2 1.4 copy-start.1
  92.3 35.8 %copy-start.3 = (f32[8,256]{1,0:T(8,128)S(1)}, f32[8,256]{1,0:T(8,128)}, u32[]{:S(2)}) copy-start(f32[8,256]{1,0:T(8,128)} %param.23) | copy-start | bytes 24580
  105.1 18.1 %all-to-all-start.3 = ((f32[16,4,256]{2,1,0:T(4,128)}), f32[16,4,256]{2,1,0:T(4,128)S(1)}, u32[]{:S(2)}, u32[]{:S(2)}) async-start(f32[16,4,256]{2,1,0:T(4,128)} %reshape.218), calls=%async_computation.3 | async-start | bytes 131072 | tf_op jit(solution)/shard_map/all_to_all | solution.py:103
  123.2 10.4 %all-to-all-start.4 = ((f32[16,4,256]{2,1,0:T(4,128)}), f32[16,4,256]{2,1,0:T(4,128)S(1)}, u32[]{:S(2)}, u32[]{:S(2)}) async-start(f32[16,4,256]{2,1,0:T(4,128)} %reshape.221), calls=%async_computation.4 | async-start | bytes 131072 | tf_op jit(solution)/shard_map/all_to_all | solution.py:110
  135.2 10.4 %all-to-all-start.5 = ((f32[16,4,256]{2,1,0:T(4,128)}), f32[16,4,256]{2,1,0:T(4,128)S(1)}, u32[]{:S(2)}, u32[]{:S(2)}) async-start(f32[16,4,256]{2,1,0:T(4,128)} %reshape.223), calls=%async_computation.5 | async-start | bytes 131072 | tf_op jit(solution)/shard_map/all_to_all | solution.py:141
  170.7 10.4 %all-to-all-start.6 = ((f32[16,4,256]{2,1,0:T(4,128)}), f32[16,4,256]{2,1,0:T(4,128)S(1)}, u32[]{:S(2)}, u32[]{:S(2)}) async-start(f32[16,4,256]{2,1,0:T(4,128)} %reshape.228), calls=%async_computation.6 | async-start | bytes 131072 | tf_op jit(solution)/shard_map/all_to_all | solution.py:103
  181.1 10.4 %all-to-all-start.7 = ((f32[16,4,256]{2,1,0:T(4,128)}), f32[16,4,256]{2,1,0:T(4,128)S(1)}, u32[]{:S(2)}, u32[]{:S(2)}) async-start(f32[16,4,256]{2,1,0:T(4,128)} %reshape.231), calls=%async_computation.7 | async-start | bytes 131072 | tf_op jit(solution)/shard_map/all_to_all | solution.py:110
where the time goes:
time: 193 us; the launch traced here: 192 us
  waiting for transfers between devices  71.4 us (37%)
  starting transfers between devices  32.6 us (17%)
  other arithmetic  28.7 us (15%)
  local copies, waits for them, and re-layouts  22.3 us (12%)
  matrix products  21.8 us (11%)
  blocking collectives  13.6 us (7%)
    all_to_all x1, waiting for transfers between devices, per_device(): lax.all_to_all(send_points, 'src', split_axis=0, concat_axis=0, tiled=True)  40.1 us
    dot_general x8, matrix products, tile_cost(): jnp.einsum('gdp,gkdq->gpkq', src_block, tgt_block, preferred_element_type...  20.7 us
    all_to_all x2, starting transfers between devices, column_pass(): lax.all_to_all(send_high.reshape(shards, capacity, cluster_size), 'src',...  14.7 us
    reduce_sum x4, other arithmetic, column_one_group(): total = jnp.sum(jnp.exp(scores - highest[:, None, :, :]), axis=1)  14.2 us
    all_to_all x1, blocking collectives, per_device(): lax.all_to_all(request_table.reshape(shards, capacity), 'src', split_axis...  13.6 us
    all_to_all x2, waiting for transfers between devices, per_device(): lax.all_to_all(send_pot, 'src', split_axis=0, concat_axis=0, tiled=True)  11.5 us
    reduce_sum x4, other arithmetic, row_one_group(): jnp.sum(jnp.exp(scores - highest[:, :, None, None]), axis=(2, 3))  10.2 us
    all_to_all x2, waiting for transfers between devices, column_pass(): lax.all_to_all(send_high.reshape(shards, capacity, cluster_size), 'src',...  10.2 us
  transfers between devices with their start and end apart: 7, of which 7 were waited for; matrix products, arithmetic and copies ran while one was open for 5% of the time, Pallas kernels for 0%

commit v1 on v0

v1 whole, which is shorter than its diff:
```python
import functools
import math

import jax
import jax.numpy as jnp
from jax import lax
from jax.experimental import pallas as pl
from jax.experimental.pallas import tpu as pltpu
from jax.sharding import PartitionSpec as P

ITERS = 2
SCALE_EPS = 0.25
KEEP_TAU = 0.8
VERY_LOW = -1e30
LOG2E = math.log2(math.e)
C = LOG2E / SCALE_EPS
OUT = -KEEP_TAU * SCALE_EPS / LOG2E
ROWS = 32
MESH = pl.DeviceIdType.MESH


def kernel(
    shards,
    x_ref, y_ref, g0_ref, far_src_ref, far_tgt_ref, owner_ref, local_ref,
    u_ref, v_ref,
    gathered, tiles, xt, far_col, norm_col, a_bc, u_acc, col_lse, b_own, b_all, send_blk, recv_blk,
    which_k, which_local,
    fwd_send, fwd_recv, bwd_send, bwd_recv, sib_send, sib_recv, small_send, small_recv,
):
    src_count, depth, points = x_ref.shape
    tgt_count = y_ref.shape[0]
    per_cluster = owner_ref.shape[1]
    half = tgt_count // 2
    group = lax.axis_index("groups")
    me = lax.axis_index("src")
    core = lax.rem(me, 2)
    chip = me // 2
    chips = shards // 2
    units = chips - 1
    place = jnp.where(lax.rem(chip, 2) == 0, chip // 2, chips - 1 - chip // 2)

    def shard_at(position):
        position = lax.rem(position + chips, chips)
        up = position < chips // 2
        return jnp.where(up, 2 * position, 2 * (chips - 1 - position) + 1) * 2 + core

    right = shard_at(place + 1)
    left = shard_at(place - 1)
    sibling = me + 1 - 2 * core

    barrier = pltpu.get_barrier_semaphore()

    @pl.loop(1, shards)
    def _(d):
        pl.semaphore_signal(
            barrier, inc=1, device_id=(group, lax.rem(me + d, shards)), device_id_type=MESH
        )

    wide = y_ref[...].astype(jnp.float32)
    tgt_norm = (0.5 * C) * jnp.sum(wide * wide, axis=1)
    b_own[0] = C * g0_ref[...] - tgt_norm
    b_all[0, me] = b_own[0]
    gathered[me] = y_ref[...]

    pl.semaphore_wait(barrier, shards - 1)

    def ring_copy(u, forward):
        step = u // 2
        parity = lax.rem(u, 2)
        part = parity if forward else 1 - parity
        owner = shard_at(place - step if forward else place + step)
        piece = gathered.at[owner, pl.ds(part * half, half)]
        sends, recvs = (fwd_send, fwd_recv) if forward else (bwd_send, bwd_recv)
        return pltpu.make_async_remote_copy(
            src_ref=piece, dst_ref=piece, send_sem=sends.at[u], recv_sem=recvs.at[u],
            device_id=(group, right if forward else left), device_id_type=MESH,
        )

    def sibling_copy(u, forward):
        step = u // 2 + 1
        parity = lax.rem(u, 2)
        part = parity if forward else 1 - parity
        owner = shard_at(place - step if forward else place + step)
        piece = gathered.at[owner, pl.ds(part * half, half)]
        slot = 1 + u if forward else 1 + units + u
        return pltpu.make_async_remote_copy(
            src_ref=piece, dst_ref=piece, send_sem=sib_send.at[slot], recv_sem=sib_recv.at[slot],
            device_id=(group, sibling), device_id_type=MESH,
        )

    def own_to_sibling():
        piece = gathered.at[me]
        return pltpu.make_async_remote_copy(
            src_ref=piece, dst_ref=piece, send_sem=sib_send.at[0], recv_sem=sib_recv.at[0],
            device_id=(group, sibling), device_id_type=MESH,
        )

    def small_copy(phase, d, src, dst):
        return pltpu.make_async_remote_copy(
            src_ref=src, dst_ref=dst,
            send_sem=small_send.at[phase, d], recv_sem=small_recv.at[phase, d],
            device_id=(group, lax.rem(me + d, shards)), device_id_type=MESH,
        )

    def spread_b(i, d):
        return small_copy(2 * i, d, b_own.at[i], b_all.at[i, me])

    def return_block(i, d):
        return small_copy(
            2 * i + 1, d, send_blk.at[i, lax.rem(me + d, shards)], recv_blk.at[i, me]
        )

    def for_peers(action):
        @pl.loop(1, shards)
        def _(d):
            action(d)

    first = min(2, units)
    for u in range(first):
        ring_copy(u, True).start()
        ring_copy(u, False).start()
    own_to_sibling().start()
    for_peers(lambda d: spread_b(0, d).start())

    @pl.loop(0, src_count)
    def _(s):
        xt[s] = x_ref[s].astype(jnp.float32).T.astype(jnp.bfloat16)

    wide = x_ref[...].astype(jnp.float32)
    src_norm = (0.5 * C) * jnp.sum(wide * wide, axis=1)
    norm_turned = src_norm.T
    far_turned = (LOG2E * far_src_ref[...] + src_norm).T
    for s in range(src_count):
        norm_col[s] = norm_turned[:, s : s + 1]
        far_col[s] = far_turned[:, s : s + 1]

    @pl.loop(0, src_count)
    def _(s):
        owners = [owner_ref[s, k] for k in range(per_cluster)]
        locals_ = [local_ref[s, k] for k in range(per_cluster)]

        @pl.loop(0, shards)
        def _(d):
            kk = jnp.int32(0)
            ll = jnp.int32(-1)
            for k in range(per_cluster):
                hit = owners[k] == d
                kk = jnp.where(hit, k, kk)
                ll = jnp.where(hit, locals_[k], ll)
            which_k[d, s] = kk
            which_local[d, s] = ll

    @pl.loop(first, units)
    def _(u):
        for forward in (True, False):
            ring_copy(u - 2, forward).wait_recv()
            ring_copy(u, forward).start()
            sibling_copy(u - 2, forward).start()

    for u in range(max(0, units - 2), units):
        for forward in (True, False):
            ring_copy(u, forward).wait_recv()
            sibling_copy(u, forward).start()

    own_to_sibling().wait()

    @pl.loop(0, units)
    def _(u):
        for forward in (True, False):
            ring_copy(u, forward).wait_send()
            sibling_copy(u, forward).wait()

    for_peers(lambda d: spread_b(0, d).wait())

    rows8 = lax.broadcasted_iota(jnp.int32, (tgt_count, points), 0)
    lanes = lax.broadcasted_iota(jnp.int32, (points, 128), 1)
    u_acc[...] = jnp.zeros_like(u_acc)
    far_tgt = LOG2E * far_tgt_ref[...] + tgt_norm

    for i in range(ITERS):

        @pl.loop(0, src_count)
        def _(s):
            if i == 0:
                for k in range(per_cluster):
                    tiles[s * per_cluster + k] = C * jnp.dot(
                        xt[s],
                        gathered[owner_ref[s, k], local_ref[s, k]],
                        preferred_element_type=jnp.float32,
                    )
            bias = [
                b_all[i, owner_ref[s, k], pl.ds(local_ref[s, k], 1), :] for k in range(per_cluster)
            ]
            for r in range(0, points, ROWS):
                here = pl.ds(r, ROWS)
                scores = [
                    tiles[s * per_cluster + k, here, :] + bias[k] for k in range(per_cluster)
                ]
                far = far_col[s, here, :]
                high = functools.reduce(jnp.maximum, scores)
                high = jnp.maximum(jnp.max(high, axis=1, keepdims=True), far)
                total = functools.reduce(jnp.add, [jnp.exp2(t - high) for t in scores])
                total = jnp.sum(total, axis=1, keepdims=True) + jnp.exp2(far - high)
                norm = norm_col[s, here, :]
                lse = high + jnp.log2(total) - norm
                a_bc[here, :] = jnp.broadcast_to(-KEEP_TAU * lse - norm, (ROWS, 128))
                if i == ITERS - 1:
                    u_acc[here, :] = jnp.where(lanes[:ROWS] == s, OUT * lse, u_acc[here, :])
            for k in range(per_cluster):
                for c in range(0, points, 128):
                    there = pl.ds(c, 128)
                    t = tiles[s * per_cluster + k, :, there] + a_bc[...]
                    high = jnp.max(t, axis=0, keepdims=True)
                    total = jnp.sum(jnp.exp2(t - high), axis=0, keepdims=True)
                    col_lse[s * per_cluster + k, :, there] = high + jnp.log2(total)

        @pl.loop(0, shards)
        def _(d):
            masks = [rows8 == which_local[d, s] for s in range(src_count)]
            rows = [
                jnp.where(masks[s], col_lse[s * per_cluster + which_k[d, s]], VERY_LOW)
                for s in range(src_count)
            ]
            high = functools.reduce(jnp.maximum, rows)
            total = functools.reduce(
                jnp.add,
                [jnp.where(masks[s], jnp.exp2(rows[s] - high), 0.0) for s in range(src_count)],
            )
            send_blk[i, d] = high + jnp.log2(jnp.maximum(total, 1.0))

        recv_blk[i, me] = send_blk[i, me]
        for_peers(lambda d: return_block(i, d).start())
        for_peers(lambda d: return_block(i, d).wait())
        best = lax.fori_loop(0, shards, lambda d, m: jnp.maximum(m, recv_blk[i, d]), far_tgt)
        total = lax.fori_loop(
            0, shards, lambda d, t: t + jnp.exp2(recv_blk[i, d] - best), jnp.exp2(far_tgt - best)
        )
        lse = best + jnp.log2(total) - tgt_norm
        if i == ITERS - 1:
            v_ref[...] = OUT * lse
        else:
            b_own[i + 1] = -KEEP_TAU * lse - tgt_norm
            b_all[i + 1, me] = b_own[i + 1]
            for_peers(lambda d: spread_b(i + 1, d).start())
            for_peers(lambda d: spread_b(i + 1, d).wait())

    u_ref[...] = u_acc[...].T[:src_count, :]


def per_device(src_points, tgt_points, g_init, far_src, far_tgt, cand_owner, cand_local):
    src_count, depth, points = src_points.shape
    tgt_count = tgt_points.shape[0]
    pairs = src_count * cand_owner.shape[1]
    shards = lax.axis_size("src")
    units = shards // 2 - 1
    f32 = jnp.float32
    scratch = [
        pltpu.VMEM((shards, tgt_count, depth, points), jnp.bfloat16),
        pltpu.VMEM((pairs, points, points), f32),
        pltpu.VMEM((src_count, points, depth), jnp.bfloat16),
        pltpu.VMEM((src_count, points, 1), f32),
        pltpu.VMEM((src_count, points, 1), f32),
        pltpu.VMEM((points, 128), f32),
        pltpu.VMEM((points, 128), f32),
        pltpu.VMEM((pairs, 1, points), f32),
        pltpu.VMEM((ITERS, tgt_count, points), f32),
        pltpu.VMEM((ITERS, shards, tgt_count, points), f32),
        pltpu.VMEM((ITERS, shards, tgt_count, points), f32),
        pltpu.VMEM((ITERS, shards, tgt_count, points), f32),
        pltpu.SMEM((shards, src_count), jnp.int32),
        pltpu.SMEM((shards, src_count), jnp.int32),
    ]
    sems = [units] * 4 + [1 + 2 * units] * 2
    scratch += [pltpu.SemaphoreType.DMA((n,)) for n in sems]
    scratch += [pltpu.SemaphoreType.DMA((2 * ITERS, shards))] * 2
    used = shards * tgt_count * points * (2 * depth + 4 * 3 * ITERS) + 4 * pairs * points * points
    vmem = pl.BlockSpec(memory_space=pltpu.VMEM)
    smem = pl.BlockSpec(memory_space=pltpu.SMEM)
    return pl.pallas_call(
        functools.partial(kernel, shards),
        out_shape=(
            jax.ShapeDtypeStruct((src_count, points), f32),
            jax.ShapeDtypeStruct((tgt_count, points), f32),
        ),
        in_specs=[vmem] * 5 + [smem] * 2,
        out_specs=(vmem, vmem),
        scratch_shapes=scratch,
        compiler_params=pltpu.CompilerParams(
            collective_id=0, has_side_effects=True, vmem_limit_bytes=used + (7 << 20)
        ),
    )(src_points, tgt_points, g_init, far_src, far_tgt, cand_owner, cand_local)


def solution(mesh):
    return jax.shard_map(
        per_device,
        mesh=mesh,
        in_specs=(
            P(("groups", "src"), None, None),
            P(("groups", "src"), None, None),
            P(("groups", "src"), None),
            P(("groups", "src"), None),
            P(("groups", "src"), None),
            P(("groups", "src"), None),
            P(("groups", "src"), None),
        ),
        out_specs=(P(("groups", "src"), None), P(("groups", "src"), None)),
        check_vma=False,
    )
```

time: 193 us -> 79.7 us (0.41)
  Pallas kernels: 0 us -> 72.1 us
  waiting for transfers between devices: 71.4 us -> 0 us
  starting transfers between devices: 32.6 us -> 0 us
  other arithmetic: 28.7 us -> 0 us
  matrix products: 21.8 us -> 0 us
  local copies, waits for them, and re-layouts: 22.3 us -> 6.55 us
  blocking collectives: 13.6 us -> 0 us
    pallas_call x0 -> x1, Pallas kernels: none -> 72.1 us  [per_device(): pl.pallas_call(functools.partial(kernel, shards), out_shape=(jax.ShapeDty...]
    all_to_all x7 -> x0, waiting for transfers between devices: 71.4 us -> none  [the longest x1 40.1 us: per_device(): lax.all_to_all(send_points, 'src', split_axis=0, concat_axis=0, tiled=True)]
    all_to_all x7 -> x0, starting transfers between devices: 32.6 us -> none  [the longest x2 14.7 us: column_pass(): lax.all_to_all(send_high.reshape(shards, capacity, cluster_size), 'src',...]
    reduce_sum x11 -> x0, other arithmetic: 25.4 us -> none  [the longest x4 14.2 us: column_one_group(): total = jnp.sum(jnp.exp(scores - highest[:, None, :, :]), axis=1)]
    dot_general x10 -> x0, matrix products: 21.8 us -> none  [the longest x8 20.7 us: tile_cost(): jnp.einsum('gdp,gkdq->gpkq', src_block, tgt_block, preferred_element_type...]
    all_to_all x1 -> x0, blocking collectives: 13.6 us -> none  [per_device(): lax.all_to_all(request_table.reshape(shards, capacity), 'src', split_axis...]
    gather x8 -> x0, local copies, waits for them, and re-layouts: 8.93 us -> none  [the longest x1 2.27 us: per_device(): chosen = flattened[slot_pos]]
    reshape x15 -> x0, local copies, waits for them, and re-layouts: 5.37 us -> none  [the longest x2 1.28 us: per_device(): send_pot = tgt_pot[safe_ids].reshape(shards, capacity, cluster_size)]
  transfers between devices with their start and end apart: 7 -> 0, of which waited for: 7 -> 0; matrix products, arithmetic and copies ran while one was open for 5% -> 0% of each run, Pallas kernels for 0% -> 0%
where the time goes in v1:
time: 79.7 us; the launch traced here: 79.3 us
  Pallas kernels  72.1 us (90%)
  local copies, waits for them, and re-layouts  6.55 us (8%)
    pallas_call x1, Pallas kernels, per_device(): pl.pallas_call(functools.partial(kernel, shards), out_shape=(jax.ShapeDty...  72.1 us
    unnamed x16, local copies, waits for them, and re-layouts  6.55 us

profile of v1, /device:TPU:0, one launch (start us, length us, event | category | flops | bytes accessed | tf_op | source)
XLA Modules:
  0.0 79.3 jit_solution(2086553405078667331)
XLA Ops:
  0.6 0.0 copy-start
  0.6 0.9 %copy-done = bf16[8,64,256]{2,1,0:T(8,128)(2,1)S(1)} copy-done((bf16[8,64,256]{2,1,0:T(8,128)(2,1)S(1)}, bf16[8,64,256]{2,1,0:T(8,128)(2,1)}, u32[]{:S(2)}) %copy-start) | copy-done | bytes 262168
  1.6 0.0 copy-start.1
  1.6 0.9 %copy-done.1 = bf16[8,64,256]{2,1,0:T(8,128)(2,1)S(1)} copy-done((bf16[8,64,256]{2,1,0:T(8,128)(2,1)S(1)}, bf16[8,64,256]{2,1,0:T(8,128)(2,1)}, u32[]{:S(2)}) %copy-start.1) | copy-done | bytes 262168
  2.5 0.0 copy-start.2
  2.5 0.7 copy-done.2
  3.2 0.0 copy-start.3
  3.2 0.7 copy-done.3
  3.9 0.0 copy-start.4
  3.9 0.7 copy-done.4
  4.6 0.0 copy-start.5
  4.6 0.7 copy-done.5
  5.3 0.0 copy-start.6
  5.3 0.7 copy-done.6
  6.0 72.1 %shard_map.86 = (f32[8,256]{1,0:T(8,128)S(1)}, f32[8,256]{1,0:T(8,128)S(1)}) custom-call(bf16[8,64,256]{2,1,0:T(8,128)(2,1)S(1)} %copy-done, bf16[8,64,256]{2,1,0:T(8,128)(2,1)S(1)} %copy-done.1, f32[8,256]{1,0:T(8,128)S(1)} %copy-done.2, f32[8,256]{1,0:T(8,128)S(1)} %copy-done.3, f32[8,256]{1,0:T(8,128)S(1)} %copy-done.4, s32[8,8]{1,0:T(8,128)S(1)} %copy-done.5, ...), custom_call_target="tpu_custom_call" | custom-call | tf_op jit(solution)/shard_map/pallas_call | solution.py:279
  78.1 0.6 copy.11
  78.7 0.6 copy.12
Async XLA Ops:
  0.6 1.0 %copy-start = (bf16[8,64,256]{2,1,0:T(8,128)(2,1)S(1)}, bf16[8,64,256]{2,1,0:T(8,128)(2,1)}, u32[]{:S(2)}) copy-start(bf16[8,64,256]{2,1,0:T(8,128)(2,1)} %x_ref.1) | copy-start | bytes 786436
  1.6 0.9 %copy-start.1 = (bf16[8,64,256]{2,1,0:T(8,128)(2,1)S(1)}, bf16[8,64,256]{2,1,0:T(8,128)(2,1)}, u32[]{:S(2)}) copy-start(bf16[8,64,256]{2,1,0:T(8,128)(2,1)} %y_ref.1) | copy-start | bytes 786436
  2.5 0.7 copy-start.2
  3.2 0.7 copy-start.3
  3.9 0.7 copy-start.4
  4.6 0.7 copy-start.5
  5.3 0.7 copy-start.6

commit v2 on v1

--- a/solution.py
+++ b/solution.py
@@ -16,19 +16,21 @@
 C = LOG2E / SCALE_EPS
 OUT = -KEEP_TAU * SCALE_EPS / LOG2E
 ROWS = 32
+VMEM_BYTES = 64 << 20
 MESH = pl.DeviceIdType.MESH
 
 
 def kernel(
-    shards,
-    x_ref, y_ref, g0_ref, far_src_ref, far_tgt_ref, owner_ref, local_ref,
+    shards, capacity, early,
+    x_hbm, y_hbm, g0_hbm, far_src_hbm, far_tgt_hbm, owner_hbm, local_hbm,
     u_ref, v_ref,
+    x_ref, g0_ref, far_src_ref, far_tgt_ref, owner_ref, local_ref, load_sem,
     gathered, tiles, xt, far_col, norm_col, a_bc, u_acc, col_lse, b_own, b_all, send_blk, recv_blk,
-    which_k, which_local,
+    which_k, which_local, slot_at, slot_src, slot_local, part_high, part_total, stage,
     fwd_send, fwd_recv, bwd_send, bwd_recv, sib_send, sib_recv, small_send, small_recv,
 ):
     src_count, depth, points = x_ref.shape
-    tgt_count = y_ref.shape[0]
+    tgt_count = g0_ref.shape[0]
     per_cluster = owner_ref.shape[1]
     half = tgt_count // 2
     group = lax.axis_index("groups")
@@ -56,12 +58,21 @@
             barrier, inc=1, device_id=(group, lax.rem(me + d, shards)), device_id_type=MESH
         )
 
-    wide = y_ref[...].astype(jnp.float32)
-    tgt_norm = (0.5 * C) * jnp.sum(wide * wide, axis=1)
-    b_own[0] = C * g0_ref[...] - tgt_norm
-    b_all[0, me] = b_own[0]
-    gathered[me] = y_ref[...]
-
+    loads = [
+        pltpu.make_async_copy(src, dst, load_sem.at[n])
+        for n, (src, dst) in enumerate((
+            (y_hbm, gathered.at[me]),
+            (g0_hbm, g0_ref),
+            (x_hbm, x_ref),
+            (owner_hbm, owner_ref),
+            (local_hbm, local_ref),
+            (far_src_hbm, far_src_ref),
+            (far_tgt_hbm, far_tgt_ref),
+        ))
+    ]
+    for load in loads:
+        load.start()
+    loads[0].wait()
     pl.semaphore_wait(barrier, shards - 1)
 
     def ring_copy(u, forward):
@@ -95,32 +106,35 @@
             device_id=(group, sibling), device_id_type=MESH,
         )
 
-    def small_copy(phase, d, src, dst):
+    def small_copy(phase, peer, src, dst):
         return pltpu.make_async_remote_copy(
             src_ref=src, dst_ref=dst,
-            send_sem=small_send.at[phase, d], recv_sem=small_recv.at[phase, d],
-            device_id=(group, lax.rem(me + d, shards)), device_id_type=MESH,
-        )
-
-    def spread_b(i, d):
-        return small_copy(2 * i, d, b_own.at[i], b_all.at[i, me])
-
-    def return_block(i, d):
-        return small_copy(
-            2 * i + 1, d, send_blk.at[i, lax.rem(me + d, shards)], recv_blk.at[i, me]
-        )
-
-    def for_peers(action):
+            send_sem=small_send.at[phase], recv_sem=small_recv.at[phase],
+            device_id=(group, peer), device_id_type=MESH,
+        )
+
+    def spread_b(i):
         @pl.loop(1, shards)
         def _(d):
-            action(d)
+            small_copy(2 * i, lax.rem(me + d, shards), b_own.at[i], b_all.at[i, me]).start()
+
+    def await_all(sem, buffer):
+        blocks = buffer.at[pl.ds(0, shards - 1)]
+        pltpu.make_async_copy(blocks, blocks, sem).wait()
 
     first = min(2, units)
     for u in range(first):
         ring_copy(u, True).start()
         ring_copy(u, False).start()
     own_to_sibling().start()
-    for_peers(lambda d: spread_b(0, d).start())
+    loads[1].wait()
+    wide = gathered[me].astype(jnp.float32)
+    tgt_norm = (0.5 * C) * jnp.sum(wide * wide, axis=1)
+    b_own[0] = C * g0_ref[...] - tgt_norm
+    b_all[0, me] = b_own[0]
+    spread_b(0)
+    for load in loads[2:]:
+        load.wait()
 
     @pl.loop(0, src_count)
     def _(s):
@@ -150,27 +164,91 @@
             which_k[d, s] = kk
             which_local[d, s] = ll
 
-    @pl.loop(first, units)
-    def _(u):
-        for forward in (True, False):
-            ring_copy(u - 2, forward).wait_recv()
-            ring_copy(u, forward).start()
-            sibling_copy(u - 2, forward).start()
-
-    for u in range(max(0, units - 2), units):
-        for forward in (True, False):
-            ring_copy(u, forward).wait_recv()
-            sibling_copy(u, forward).start()
-
-    own_to_sibling().wait()
-
-    @pl.loop(0, units)
-    def _(u):
-        for forward in (True, False):
-            ring_copy(u, forward).wait_send()
-            sibling_copy(u, forward).wait()
-
-    for_peers(lambda d: spread_b(0, d).wait())
+    @pl.loop(0, shards if early else 0)
+    def _(d):
+        count = jnp.int32(0)
+        sources = [jnp.int32(0)] * capacity
+        locals_ = [jnp.int32(0)] * capacity
+        for s in range(src_count):
+            ll = which_local[d, s]
+            slot_at[d, s] = d * capacity + jnp.minimum(count, capacity - 1)
+            for c in range(capacity):
+                take = (ll >= 0) & (count == c)
+                sources[c] = jnp.where(take, s, sources[c])
+                locals_[c] = jnp.where(take, ll, locals_[c])
+            count = count + jnp.where(ll >= 0, 1, 0)
+        for c in range(capacity):
+            slot_src[d, c] = sources[c]
+            slot_local[d, c] = locals_[c]
+
+    def row_parts(d):
+        if early:
+            stage[...] = gathered[d]
+
+            @pl.loop(0, capacity)
+            def _(c):
+                slot = d * capacity + c
+                local = slot_local[d, c]
+                bias = b_all[0, d, pl.ds(local, 1), :]
+                t = C * jnp.dot(
+                    xt[slot_src[d, c]], stage[local], preferred_element_type=jnp.float32
+                )
+                tiles[slot] = t
+                t = t + bias
+                lanes_of = [t[:, c : c + 128] for c in range(0, points, 128)]
+                high = functools.reduce(jnp.maximum, lanes_of)
+                part_high[slot] = high
+                part_total[slot] = functools.reduce(
+                    jnp.add, [jnp.exp2(p - high) for p in lanes_of]
+                )
+
+    def across(owner):
+        return owner + 1 - 2 * core
+
+    steps = (units - 1) // 2
+
+    @pl.loop(0, steps)
+    def _(t):
+        for h in range(2):
+            u = 2 * t + h
+            for forward in (True, False):
+                ring_copy(u, forward).wait_recv()
+
+                @pl.when(u + 2 < units)
+                def _():
+                    ring_copy(u + 2, forward).start()
+
+                sibling_copy(u, forward).start()
+
+        @pl.when(t == 0)
+        def _():
+            await_all(small_recv.at[0], b_all.at[0])
+            own_to_sibling().wait_recv()
+            row_parts(me)
+            row_parts(sibling)
+
+        @pl.when(t > 0)
+        def _():
+            for forward in (True, False):
+                for h in range(2):
+                    sibling_copy(2 * t - 2 + h, forward).wait_recv()
+                row_parts(across(shard_at(place - t if forward else place + t)))
+
+        row_parts(shard_at(place - t - 1))
+        row_parts(shard_at(place + t + 1))
+
+    last = units - 1
+    for forward in (True, False):
+        ring_copy(last, forward).wait_recv()
+        sibling_copy(last, forward).start()
+    for forward in (True, False):
+        for h in range(2):
+            sibling_copy(2 * steps - 2 + h, forward).wait_recv()
+        row_parts(across(shard_at(place - steps if forward else place + steps)))
+    row_parts(shard_at(place + steps + 1))
+    for forward in (True, False):
+        sibling_copy(last, forward).wait_recv()
+    row_parts(across(shard_at(place + steps + 1)))
 
     rows8 = lax.broadcasted_iota(jnp.int32, (tgt_count, points), 0)
     lanes = lax.broadcasted_iota(jnp.int32, (points, 128), 1)
@@ -181,9 +259,13 @@
 
         @pl.loop(0, src_count)
         def _(s):
-            if i == 0:
+            if early:
+                at = [slot_at[owner_ref[s, k], s] for k in range(per_cluster)]
+            else:
+                at = [s * per_cluster + k for k in range(per_cluster)]
+            if i == 0 and not early:
                 for k in range(per_cluster):
-                    tiles[s * per_cluster + k] = C * jnp.dot(
+                    tiles[at[k]] = C * jnp.dot(
                         xt[s],
                         gathered[owner_ref[s, k], local_ref[s, k]],
                         preferred_element_type=jnp.float32,
@@ -193,13 +275,23 @@
             ]
             for r in range(0, points, ROWS):
                 here = pl.ds(r, ROWS)
-                scores = [
-                    tiles[s * per_cluster + k, here, :] + bias[k] for k in range(per_cluster)
-                ]
                 far = far_col[s, here, :]
-                high = functools.reduce(jnp.maximum, scores)
-                high = jnp.maximum(jnp.max(high, axis=1, keepdims=True), far)
-                total = functools.reduce(jnp.add, [jnp.exp2(t - high) for t in scores])
+                if i == 0 and early:
+                    highs = [part_high[at[k], here, :] for k in range(per_cluster)]
+                    high = functools.reduce(jnp.maximum, highs)
+                    high = jnp.maximum(jnp.max(high, axis=1, keepdims=True), far)
+                    total = functools.reduce(
+                        jnp.add,
+                        [
+                            part_total[at[k], here, :] * jnp.exp2(highs[k] - high)
+                            for k in range(per_cluster)
+                        ],
+                    )
+                else:
+                    scores = [tiles[at[k], here, :] + bias[k] for k in range(per_cluster)]
+                    high = functools.reduce(jnp.maximum, scores)
+                    high = jnp.maximum(jnp.max(high, axis=1, keepdims=True), far)
+                    total = functools.reduce(jnp.add, [jnp.exp2(t - high) for t in scores])
                 total = jnp.sum(total, axis=1, keepdims=True) + jnp.exp2(far - high)
                 norm = norm_col[s, here, :]
                 lse = high + jnp.log2(total) - norm
@@ -209,7 +301,7 @@
             for k in range(per_cluster):
                 for c in range(0, points, 128):
                     there = pl.ds(c, 128)
-                    t = tiles[s * per_cluster + k, :, there] + a_bc[...]
+                    t = tiles[at[k], :, there] + a_bc[...]
                     high = jnp.max(t, axis=0, keepdims=True)
                     total = jnp.sum(jnp.exp2(t - high), axis=0, keepdims=True)
                     col_lse[s * per_cluster + k, :, there] = high + jnp.log2(total)
@@ -228,9 +320,13 @@
             )
             send_blk[i, d] = high + jnp.log2(jnp.maximum(total, 1.0))
 
+        @pl.loop(1, shards)
+        def _(d):
+            peer = lax.rem(me + d, shards)
+            small_copy(2 * i + 1, peer, send_blk.at[i, peer], recv_blk.at[i, me]).start()
+
         recv_blk[i, me] = send_blk[i, me]
-        for_peers(lambda d: return_block(i, d).start())
-        for_peers(lambda d: return_block(i, d).wait())
+        await_all(small_recv.at[2 * i + 1], recv_blk.at[i])
         best = lax.fori_loop(0, shards, lambda d, m: jnp.maximum(m, recv_blk[i, d]), far_tgt)
         total = lax.fori_loop(
             0, shards, lambda d, t: t + jnp.exp2(recv_blk[i, d] - best), jnp.exp2(far_tgt - best)
@@ -241,10 +337,21 @@
         else:
             b_own[i + 1] = -KEEP_TAU * lse - tgt_norm
             b_all[i + 1, me] = b_own[i + 1]
-            for_peers(lambda d: spread_b(i + 1, d).start())
-            for_peers(lambda d: spread_b(i + 1, d).wait())
+            spread_b(i + 1)
+            await_all(small_recv.at[2 * i + 2], b_all.at[i + 1])
 
     u_ref[...] = u_acc[...].T[:src_count, :]
+
+    own_to_sibling().wait_send()
+
+    @pl.loop(0, units)
+    def _(u):
+        for forward in (True, False):
+            ring_copy(u, forward).wait_send()
+            sibling_copy(u, forward).wait_send()
+
+    for phase in range(2 * ITERS):
+        await_all(small_send.at[phase], recv_blk.at[0])
 
 
 def per_device(src_points, tgt_points, g_init, far_src, far_tgt, cand_owner, cand_local):
@@ -253,8 +360,18 @@
     pairs = src_count * cand_owner.shape[1]
     shards = lax.axis_size("src")
     units = shards // 2 - 1
+    capacity = max(2, min(src_count // 2, 2 * pairs // shards))
+    early = shards * capacity <= pairs and units >= 3
+    parts = pairs if early else 1
     f32 = jnp.float32
     scratch = [
+        pltpu.VMEM(src_points.shape, jnp.bfloat16),
+        pltpu.VMEM(g_init.shape, f32),
+        pltpu.VMEM(far_src.shape, f32),
+        pltpu.VMEM(far_tgt.shape, f32),
+        pltpu.SMEM(cand_owner.shape, jnp.int32),
+        pltpu.SMEM(cand_local.shape, jnp.int32),
+        pltpu.SemaphoreType.DMA((7,)),
         pltpu.VMEM((shards, tgt_count, depth, points), jnp.bfloat16),
         pltpu.VMEM((pairs, points, points), f32),
         pltpu.VMEM((src_count, points, depth), jnp.bfloat16),
@@ -270,23 +387,25 @@
         pltpu.SMEM((shards, src_count), jnp.int32),
         pltpu.SMEM((shards, src_count), jnp.int32),
     ]
+    scratch += [pltpu.SMEM((shards, n), jnp.int32) for n in (src_count, capacity, capacity)]
+    scratch += [pltpu.VMEM((parts, points, 128), f32)] * 2
+    scratch += [pltpu.VMEM(tgt_points.shape, jnp.bfloat16)]
     sems = [units] * 4 + [1 + 2 * units] * 2
     scratch += [pltpu.SemaphoreType.DMA((n,)) for n in sems]
-    scratch += [pltpu.SemaphoreType.DMA((2 * ITERS, shards))] * 2
-    used = shards * tgt_count * points * (2 * depth + 4 * 3 * ITERS) + 4 * pairs * points * points
+    scratch += [pltpu.SemaphoreType.DMA((2 * ITERS,))] * 2
     vmem = pl.BlockSpec(memory_space=pltpu.VMEM)
-    smem = pl.BlockSpec(memory_space=pltpu.SMEM)
+    hbm = pl.BlockSpec(memory_space=pltpu.HBM)
     return pl.pallas_call(
-        functools.partial(kernel, shards),
+        functools.partial(kernel, shards, capacity, early),
         out_shape=(
             jax.ShapeDtypeStruct((src_count, points), f32),
             jax.ShapeDtypeStruct((tgt_count, points), f32),
         ),
-        in_specs=[vmem] * 5 + [smem] * 2,
+        in_specs=[hbm] * 7,
         out_specs=(vmem, vmem),
         scratch_shapes=scratch,
         compiler_params=pltpu.CompilerParams(
-            collective_id=0, has_side_effects=True, vmem_limit_bytes=used + (7 << 20)
+            collective_id=0, has_side_effects=True, vmem_limit_bytes=VMEM_BYTES
         ),
     )(src_points, tgt_points, g_init, far_src, far_tgt, cand_owner, cand_local)
 

time: 79.7 us -> 73.8 us (0.926)
  local copies, waits for them, and re-layouts: 6.55 us -> 1.9 us
  Pallas kernels: 72.1 us -> 71.1 us
    unnamed x16 -> x4, local copies, waits for them, and re-layouts: 6.55 us -> 1.9 us
    pallas_call x1, Pallas kernels: 72.1 us -> 71.1 us  [per_device(): pl.pallas_call(functools.partial(kernel, shards, capacity, early), out_sh...]
where the time goes in v2:
time: 73.8 us; the launch traced here: 73.7 us
  Pallas kernels  71.1 us (96%)
  local copies, waits for them, and re-layouts  1.9 us (3%)
    pallas_call x1, Pallas kernels, per_device(): pl.pallas_call(functools.partial(kernel, shards, capacity, early), out_sh...  71.1 us
    unnamed x4, local copies, waits for them, and re-layouts  1.9 us

profile of v2, /device:TPU:0, one launch (start us, length us, event | category | flops | bytes accessed | tf_op | source)
XLA Modules:
  0.0 73.7 jit_solution(13024710613980061600)
XLA Ops:
  0.6 71.1 %shard_map.86 = (f32[8,256]{1,0:T(8,128)}, f32[8,256]{1,0:T(8,128)}) custom-call(bf16[8,64,256]{2,1,0:T(8,128)(2,1)} %x_hbm.1, bf16[8,64,256]{2,1,0:T(8,128)(2,1)} %y_hbm.1, f32[8,256]{1,0:T(8,128)} %g0_hbm.1, f32[8,256]{1,0:T(8,128)} %far_src_hbm.1, f32[8,256]{1,0:T(8,128)} %far_tgt_hbm.1, s32[8,8]{1,0:T(8,128)} %owner_hbm.1, s32[8,8]{1,0:T(8,128)} %local_hbm.1), custom_call_target="tpu_custom_call" | custom-call | tf_op jit(solution)/shard_map/pallas_call | solution.py:398
  71.7 0.0 copy-start
  71.8 1.3 %copy.11 = f32[8,256]{1,0:T(8,128)} copy(f32[8,256]{1,0:T(8,128)} %get-tuple-element.4) | data formatting | bytes 16384
  73.1 0.0 copy-done
  73.1 0.6 copy.12
Async XLA Ops:
  71.7 1.3 %copy-start = (f32[8,256]{1,0:T(8,128)S(1)}, f32[8,256]{1,0:T(8,128)}, u32[]{:S(2)}) copy-start(f32[8,256]{1,0:T(8,128)} %get-tuple-element.5) | copy-start | bytes 24580

commit v3 on v2

--- a/solution.py
+++ b/solution.py
@@ -15,7 +15,7 @@
 LOG2E = math.log2(math.e)
 C = LOG2E / SCALE_EPS
 OUT = -KEEP_TAU * SCALE_EPS / LOG2E
-ROWS = 32
+ROWS = 16
 VMEM_BYTES = 64 << 20
 MESH = pl.DeviceIdType.MESH
 
@@ -26,7 +26,7 @@
     u_ref, v_ref,
     x_ref, g0_ref, far_src_ref, far_tgt_ref, owner_ref, local_ref, load_sem,
     gathered, tiles, xt, far_col, norm_col, a_bc, u_acc, col_lse, b_own, b_all, send_blk, recv_blk,
-    which_k, which_local, slot_at, slot_src, slot_local, part_high, part_total, stage,
+    which_k, which_local, slot_at, slot_src, slot_local, slot_row, row_high, row_total, part_high, part_total, stage,
     fwd_send, fwd_recv, bwd_send, bwd_recv, sib_send, sib_recv, small_send, small_recv,
 ):
     src_count, depth, points = x_ref.shape
@@ -145,8 +145,8 @@
     norm_turned = src_norm.T
     far_turned = (LOG2E * far_src_ref[...] + src_norm).T
     for s in range(src_count):
-        norm_col[s] = norm_turned[:, s : s + 1]
-        far_col[s] = far_turned[:, s : s + 1]
+        norm_col[s] = jnp.broadcast_to(norm_turned[:, s : s + 1], (points, 128))
+        far_col[s] = jnp.broadcast_to(far_turned[:, s : s + 1], (points, 128))
 
     @pl.loop(0, src_count)
     def _(s):
@@ -168,7 +168,7 @@
     def _(d):
         count = jnp.int32(0)
         sources = [jnp.int32(0)] * capacity
-        locals_ = [jnp.int32(0)] * capacity
+        locals_ = [jnp.int32(-1)] * capacity
         for s in range(src_count):
             ll = which_local[d, s]
             slot_at[d, s] = d * capacity + jnp.minimum(count, capacity - 1)
@@ -179,7 +179,8 @@
             count = count + jnp.where(ll >= 0, 1, 0)
         for c in range(capacity):
             slot_src[d, c] = sources[c]
-            slot_local[d, c] = locals_[c]
+            slot_local[d, c] = jnp.maximum(locals_[c], 0)
+            slot_row[d, c] = locals_[c]
 
     def row_parts(d):
         if early:
@@ -254,6 +255,15 @@
     lanes = lax.broadcasted_iota(jnp.int32, (points, 128), 1)
     u_acc[...] = jnp.zeros_like(u_acc)
     far_tgt = LOG2E * far_tgt_ref[...] + tgt_norm
+
+    def column_lse(tile, s):
+        pieces = []
+        for c in range(0, points, 128):
+            t = tile[:, pl.ds(c, 128)] + a_bc[s]
+            high = jnp.max(t, axis=0, keepdims=True)
+            total = jnp.sum(jnp.exp2(t - high), axis=0, keepdims=True)
+            pieces.append(high + jnp.log2(total))
+        return jnp.concatenate(pieces, axis=1)
 
     for i in range(ITERS):
 
@@ -275,11 +285,9 @@
             ]
             for r in range(0, points, ROWS):
                 here = pl.ds(r, ROWS)
-                far = far_col[s, here, :]
                 if i == 0 and early:
                     highs = [part_high[at[k], here, :] for k in range(per_cluster)]
                     high = functools.reduce(jnp.maximum, highs)
-                    high = jnp.maximum(jnp.max(high, axis=1, keepdims=True), far)
                     total = functools.reduce(
                         jnp.add,
                         [
@@ -288,42 +296,54 @@
                         ],
                     )
                 else:
-                    scores = [tiles[at[k], here, :] + bias[k] for k in range(per_cluster)]
+                    scores = [
+                        tiles[at[k], here, pl.ds(c, 128)] + bias[k][:, c : c + 128]
+                        for k in range(per_cluster)
+                        for c in range(0, points, 128)
+                    ]
                     high = functools.reduce(jnp.maximum, scores)
-                    high = jnp.maximum(jnp.max(high, axis=1, keepdims=True), far)
                     total = functools.reduce(jnp.add, [jnp.exp2(t - high) for t in scores])
-                total = jnp.sum(total, axis=1, keepdims=True) + jnp.exp2(far - high)
-                norm = norm_col[s, here, :]
-                lse = high + jnp.log2(total) - norm
-                a_bc[here, :] = jnp.broadcast_to(-KEEP_TAU * lse - norm, (ROWS, 128))
-                if i == ITERS - 1:
-                    u_acc[here, :] = jnp.where(lanes[:ROWS] == s, OUT * lse, u_acc[here, :])
-            for k in range(per_cluster):
-                for c in range(0, points, 128):
-                    there = pl.ds(c, 128)
-                    t = tiles[at[k], :, there] + a_bc[...]
-                    high = jnp.max(t, axis=0, keepdims=True)
-                    total = jnp.sum(jnp.exp2(t - high), axis=0, keepdims=True)
-                    col_lse[s * per_cluster + k, :, there] = high + jnp.log2(total)
-
-        @pl.loop(0, shards)
-        def _(d):
-            masks = [rows8 == which_local[d, s] for s in range(src_count)]
-            rows = [
-                jnp.where(masks[s], col_lse[s * per_cluster + which_k[d, s]], VERY_LOW)
-                for s in range(src_count)
-            ]
+                row_high[here, :] = high
+                row_total[here, :] = total
+            far = far_col[s]
+            norm = norm_col[s]
+            high = row_high[...]
+            top = jnp.maximum(
+                jnp.broadcast_to(jnp.max(high, axis=1, keepdims=True), high.shape), far
+            )
+            total = row_total[...] * jnp.exp2(high - top)
+            total = jnp.broadcast_to(jnp.sum(total, axis=1, keepdims=True), high.shape)
+            lse = top + jnp.log2(total + jnp.exp2(far - top)) - norm
+            a_bc[s] = -KEEP_TAU * lse - norm
+            if i == ITERS - 1:
+                u_acc[...] = jnp.where(lanes == s, OUT * lse, u_acc[...])
+            if not early:
+                for k in range(per_cluster):
+                    col_lse[s * per_cluster + k] = column_lse(tiles.at[at[k]], s)
+
+        @pl.loop(1, shards + 1)
+        def _(o):
+            d = lax.rem(me + o, shards)
+            if early:
+                masks = [rows8 == slot_row[d, c] for c in range(capacity)]
+                parts = [
+                    column_lse(tiles.at[d * capacity + c], slot_src[d, c]) for c in range(capacity)
+                ]
+            else:
+                masks = [rows8 == which_local[d, s] for s in range(src_count)]
+                parts = [
+                    col_lse[s * per_cluster + which_k[d, s]] for s in range(src_count)
+                ]
+            rows = [jnp.where(m, p, VERY_LOW) for m, p in zip(masks, parts)]
             high = functools.reduce(jnp.maximum, rows)
             total = functools.reduce(
-                jnp.add,
-                [jnp.where(masks[s], jnp.exp2(rows[s] - high), 0.0) for s in range(src_count)],
+                jnp.add, [jnp.where(m, jnp.exp2(p - high), 0.0) for m, p in zip(masks, rows)]
             )
             send_blk[i, d] = high + jnp.log2(jnp.maximum(total, 1.0))
 
-        @pl.loop(1, shards)
-        def _(d):
-            peer = lax.rem(me + d, shards)
-            small_copy(2 * i + 1, peer, send_blk.at[i, peer], recv_blk.at[i, me]).start()
+            @pl.when(o < shards)
+            def _():
+                small_copy(2 * i + 1, d, send_blk.at[i, d], recv_blk.at[i, me]).start()
 
         recv_blk[i, me] = send_blk[i, me]
         await_all(small_recv.at[2 * i + 1], recv_blk.at[i])
@@ -375,9 +395,9 @@
         pltpu.VMEM((shards, tgt_count, depth, points), jnp.bfloat16),
         pltpu.VMEM((pairs, points, points), f32),
         pltpu.VMEM((src_count, points, depth), jnp.bfloat16),
-        pltpu.VMEM((src_count, points, 1), f32),
-        pltpu.VMEM((src_count, points, 1), f32),
-        pltpu.VMEM((points, 128), f32),
+        pltpu.VMEM((src_count, points, 128), f32),
+        pltpu.VMEM((src_count, points, 128), f32),
+        pltpu.VMEM((src_count, points, 128), f32),
         pltpu.VMEM((points, 128), f32),
         pltpu.VMEM((pairs, 1, points), f32),
         pltpu.VMEM((ITERS, tgt_count, points), f32),
@@ -387,7 +407,8 @@
         pltpu.SMEM((shards, src_count), jnp.int32),
         pltpu.SMEM((shards, src_count), jnp.int32),
     ]
-    scratch += [pltpu.SMEM((shards, n), jnp.int32) for n in (src_count, capacity, capacity)]
+    scratch += [pltpu.SMEM((shards, n), jnp.int32) for n in (src_count,) + 3 * (capacity,)]
+    scratch += [pltpu.VMEM((points, 128), f32)] * 2
     scratch += [pltpu.VMEM((parts, points, 128), f32)] * 2
     scratch += [pltpu.VMEM(tgt_points.shape, jnp.bfloat16)]
     sems = [units] * 4 + [1 + 2 * units] * 2

time: 73.8 us -> 64.8 us (0.88)
  Pallas kernels: 71.1 us -> 62.1 us
    pallas_call x1, Pallas kernels: 71.1 us -> 62.1 us  [per_device(): pl.pallas_call(functools.partial(kernel, shards, capacity, early), out_sh...]
where the time goes in v3:
time: 64.8 us; the launch traced here: 64.7 us
  Pallas kernels  62.1 us (96%)
  local copies, waits for them, and re-layouts  1.9 us (3%)
  between operations  0.65 us (1%)
    pallas_call x1, Pallas kernels, per_device(): pl.pallas_call(functools.partial(kernel, shards, capacity, early), out_sh...  62.1 us
    unnamed x4, local copies, waits for them, and re-layouts  1.9 us

profile of v3, /device:TPU:0, one launch (start us, length us, event | category | flops | bytes accessed | tf_op | source)
XLA Modules:
  0.0 64.7 jit_solution(9375371456503361103)
XLA Ops:
  0.6 62.1 %shard_map.86 = (f32[8,256]{1,0:T(8,128)}, f32[8,256]{1,0:T(8,128)}) custom-call(bf16[8,64,256]{2,1,0:T(8,128)(2,1)} %x_hbm.1, bf16[8,64,256]{2,1,0:T(8,128)(2,1)} %y_hbm.1, f32[8,256]{1,0:T(8,128)} %g0_hbm.1, f32[8,256]{1,0:T(8,128)} %far_src_hbm.1, f32[8,256]{1,0:T(8,128)} %far_tgt_hbm.1, s32[8,8]{1,0:T(8,128)} %owner_hbm.1, s32[8,8]{1,0:T(8,128)} %local_hbm.1), custom_call_target="tpu_custom_call" | custom-call | tf_op jit(solution)/shard_map/pallas_call | solution.py:419
  62.8 0.0 copy-start
  62.8 1.3 %copy.11 = f32[8,256]{1,0:T(8,128)} copy(f32[8,256]{1,0:T(8,128)} %get-tuple-element.4) | data formatting | bytes 16384
  64.1 0.0 copy-done
  64.1 0.6 copy.12
Async XLA Ops:
  62.8 1.3 %copy-start = (f32[8,256]{1,0:T(8,128)S(1)}, f32[8,256]{1,0:T(8,128)}, u32[]{:S(2)}) copy-start(f32[8,256]{1,0:T(8,128)} %get-tuple-element.5) | copy-start | bytes 24580
